TPU v7x, 512 devices: a whole 4x8x8 slice. The times are simulated.
512 devices in a mesh: wide: 32 (over y, z_hi, core), ctx: 16 (over x, z_lo).
Axes of the slice: x: 4, y: 8, z: 8 (z_hi: 2, z_lo: 4; z = z_hi * 4 + z_lo), core: 2. Of those that a mesh axis runs over, the one named last changes fastest.
Arguments:
- q_pol: bfloat16 [32, 2048, 2048], P('wide', 'ctx'), may hold values from -24 to 24
- k_pol: bfloat16 [32, 2048, 512], P('wide', 'ctx'), may hold values from -24 to 24
- v_pol: bfloat16 [32, 2048, 512], P('wide', 'ctx'), may hold values from -6 to 6
- d_out: bfloat16 [32, 2048, 2048], P('wide', 'ctx'), may hold values from -6 to 6
- h_ref: bfloat16 [32, 2048, 4096], P('wide', 'ctx'), may hold values from -400 to 400
- norm_gain: bfloat16 [4096], replicated, may hold values from 0.5 to 1.5
- w_kv_ref: bfloat16 [4096, 1024], P('wide'), may hold values from -0.09375 to 0.09375
- lengths: int32 [32, 4], P('wide'), may hold values from 1 to 1024, 2048 in all within a row
- block_map: int32 [16, 2], replicated, may hold values from 0 to 31, as said below
Outputs:
- d_query: float32 [32, 2048, 2048], P('wide', 'ctx')
- d_key: float32 [32, 2048, 512], P('wide', 'ctx')
- d_value: float32 [32, 2048, 512], P('wide', 'ctx')
- k_ref: bfloat16 [32, 2048, 512], P('wide', 'ctx')
- v_ref: bfloat16 [32, 2048, 512], P('wide', 'ctx')
Inputs may be any that keep to these rules, and one draw needn't show every extreme that they name: Each row of block_map is j and 31 - j; its first column holds each of 0 to 15 once.
All inputs are finite; a program needn't handle non-finite values.
Results may differ from a plain program's by a relative error of at most 0.018.
Values may be sent and summed in bfloat16 or wider, within the bound.
A program may use at most 128 MiB of HBM per device.

v0:
```python
import jax
import jax.numpy as jnp
from jax import lax
from jax.sharding import PartitionSpec as P

HEAD_DIM = 128


def combine_rows(left, right):
    top = jnp.maximum(left[0], right[0])
    total = left[1] * jnp.exp(left[0] - top) + right[1] * jnp.exp(right[0] - top)
    return (top, total)


def body(q_pol, k_pol, v_pol, d_out, h_ref, norm_gain, w_kv_ref, lengths, block_map):
    tok_rows = q_pol.shape[1]
    half_rows = tok_rows // 2
    ctx_count = lax.axis_size("ctx")
    all_count = tok_rows * ctx_count
    block_count = 2 * ctx_count
    key_width = k_pol.shape[2]
    kv_count = key_width // HEAD_DIM
    group_size = q_pol.shape[2] // key_width
    score_scale = HEAD_DIM ** (-0.5)
    own_index = lax.axis_index("ctx")
    flat_table = block_map.reshape(-1)
    block_range = jnp.arange(block_count, dtype=jnp.int32)
    slot_of_block = jnp.sum(
        jnp.where(flat_table[None, :] == block_range[:, None], block_range[None, :], 0), axis=1
    )
    own_pair = lax.dynamic_slice_in_dim(block_map, own_index, 1, 0)[0]
    row_offsets = jnp.arange(half_rows, dtype=jnp.int32)
    lower_places = own_pair[0] * half_rows + row_offsets
    upper_places = own_pair[1] * half_rows + row_offsets
    key_places = jnp.arange(all_count, dtype=jnp.int32)
    doc_ends = jnp.cumsum(lengths[0])

    def documents(places):
        return jnp.sum((places[:, None] >= doc_ends[None, :]).astype(jnp.int32), axis=1)

    key_segment = documents(key_places)
    keys_all, values_all = (
        lax.all_gather(k_pol, "ctx", axis=1, tiled=True),
        lax.all_gather(v_pol, "ctx", axis=1, tiled=True),
    )

    def to_places(stored):
        blocks = stored[0].reshape(block_count, half_rows, key_width)
        return jnp.take(blocks, slot_of_block, axis=0).reshape(all_count, kv_count, HEAD_DIM)

    keys_pos = to_places(keys_all)
    values_pos = to_places(values_all)
    queries = q_pol[0].reshape(tok_rows, kv_count, group_size, HEAD_DIM)
    grads = d_out[0].reshape(tok_rows, kv_count, group_size, HEAD_DIM)

    def attend(q_rows, o_rows, row_places, key_count):
        k_part = keys_pos[:key_count]
        v_part = values_pos[:key_count]
        visible = (key_places[None, :key_count] <= row_places[:, None]) & (
            key_segment[None, :key_count] == documents(row_places)[:, None]
        )
        scores = (
            jnp.einsum("tkgd,ckd->kgtc", q_rows, k_part, preferred_element_type=jnp.float32)
            * score_scale
        )
        scores = jnp.where(visible[None, None], scores, jnp.float32(-1e30))
        row_top, row_total = lax.reduce(
            (scores, jnp.ones_like(scores)),
            (jnp.float32(-1e30), jnp.float32(0.0)),
            combine_rows,
            (3,),
        )
        row_top = row_top[..., None]
        row_total = row_total[..., None]
        probs_low = (jnp.exp(scores - row_top) / row_total).astype(jnp.bfloat16)
        d_probs = jnp.einsum("tkgd,ckd->kgtc", o_rows, v_part, preferred_element_type=jnp.float32)
        mixed = jnp.einsum("kgtc,ckd->kgtd", probs_low, v_part, preferred_element_type=jnp.float32)
        row_delta = jnp.einsum(
            "kgtd,tkgd->kgt", mixed, o_rows.astype(jnp.float32), precision=lax.Precision.HIGHEST
        )[..., None]
        d_scores = (jnp.exp(scores - row_top) / row_total * (d_probs - row_delta)).astype(
            jnp.bfloat16
        )
        d_rows = (
            jnp.einsum("kgtc,ckd->tkgd", d_scores, k_part, preferred_element_type=jnp.float32)
            * score_scale
        )
        return (d_rows, d_scores, probs_low)

    lower_q = queries[:half_rows]
    upper_q = queries[half_rows:]
    lower_o = grads[:half_rows]
    upper_o = grads[half_rows:]
    lower_dq, lower_ds, lower_pl = attend(lower_q, lower_o, lower_places, all_count // 2)
    upper_dq, upper_ds, upper_pl = attend(upper_q, upper_o, upper_places, all_count)
    d_query = jnp.concatenate([lower_dq, upper_dq], axis=0).reshape(tok_rows, -1)[None]

    def term_pair(d_scores, probs_low, q_rows, o_rows):
        key_part = (
            jnp.einsum("kgtc,tkgd->ckd", d_scores, q_rows, preferred_element_type=jnp.float32)
            * score_scale
        )
        value_part = jnp.einsum(
            "kgtc,tkgd->ckd", probs_low, o_rows, preferred_element_type=jnp.float32
        )
        rows = key_part.shape[0]
        return (key_part.reshape(rows, key_width), value_part.reshape(rows, key_width))

    up_key, up_value = term_pair(upper_ds, upper_pl, upper_q, upper_o)
    lo_key, lo_value = term_pair(lower_ds, lower_pl, lower_q, lower_o)
    padding = ((0, all_count // 2), (0, 0))

    def to_stored(placed):
        blocks = placed.reshape(block_count, half_rows, key_width)
        return jnp.take(blocks, flat_table, axis=0).reshape(all_count, key_width)[None]

    key_terms = to_stored(up_key + jnp.pad(lo_key, padding))
    value_terms = to_stored(up_value + jnp.pad(lo_value, padding))
    d_key, d_value = (
        lax.psum_scatter(
            key_terms.astype(jnp.bfloat16), "ctx", scatter_dimension=1, tiled=True
        ).astype(jnp.float32),
        lax.psum_scatter(
            value_terms.astype(jnp.bfloat16), "ctx", scatter_dimension=1, tiled=True
        ).astype(jnp.float32),
    )
    activations = h_ref[0].astype(jnp.float32)
    mean_square = jnp.mean(activations * activations, axis=-1, keepdims=True)
    normed = (activations * lax.rsqrt(mean_square + 1e-05) * norm_gain.astype(jnp.float32)).astype(
        jnp.bfloat16
    )
    projected = jnp.dot(
        normed,
        lax.all_gather(w_kv_ref, "wide", axis=0, tiled=True),
        preferred_element_type=jnp.float32,
    )
    projected = projected.astype(jnp.bfloat16)
    return (d_query, d_key, d_value, projected[None, :, :key_width], projected[None, :, key_width:])


def solution(mesh):
    return jax.shard_map(
        body,
        mesh=mesh,
        in_specs=(
            P("wide", "ctx", None),
            P("wide", "ctx", None),
            P("wide", "ctx", None),
            P("wide", "ctx", None),
            P("wide", "ctx", None),
            P(),
            P("wide", None),
            P("wide", None),
            P(),
        ),
        out_specs=(
            P("wide", "ctx", None),
            P("wide", "ctx", None),
            P("wide", "ctx", None),
            P("wide", "ctx", None),
            P("wide", "ctx", None),
        ),
        check_vma=False,
    )
```

profile of v0, /device:TPU:16, one launch (start us, length us, event | category | flops | bytes accessed | tf_op | source)
XLA Modules:
  0.0 550.2 jit_solution(6753983589733949058)
XLA Ops:
  21.1 84.8 %all-gather.6.cloned.1.call-done = bf16[1,2048,512]{2,1,0:T(8,128)(2,1)} async-done(((bf16[1,128,512]{2,1,0:T(8,128)(2,1)}), bf16[1,2048,512]{2,1,0:T(8,128)(2,1)}) %all-gather.6.cloned.1.call-update) | async-done | bytes 2097168 | tf_op jit(solution)/shard_map/all_gather | solution.py:44
  108.2 88.0 %all-gather.4.cloned.1.call-done = bf16[1,2048,512]{2,1,0:T(8,128)(2,1)} async-done(((bf16[1,128,512]{2,1,0:T(8,128)(2,1)}), bf16[1,2048,512]{2,1,0:T(8,128)(2,1)}) %all-gather.4.cloned.1.call-update) | async-done | bytes 2097168 | tf_op jit(solution)/shard_map/all_gather | solution.py:43
  196.2 3.6 gather_fusion
  199.8 3.3 broadcast_select_fusion.1
  210.3 4.0 reshape.241
  222.4 2.6 fusion.30
  227.8 4.2 fusion.4
  235.2 3.0 copy.52
  238.2 2.9 copy.56
  242.3 4.2 fusion.2
  246.6 3.0 fusion.11
  249.6 4.4 fusion.9
  256.2 7.1 %fusion.1 = bf16[4,4,64,2048]{3,2,1,0:T(8,128)(2,1)S(1)} fusion(f32[4,4,64]{2,1,0:T(4,128)S(1)} %copy.77, bf16[2048,4,128,1]{2,1,0,3:T(4,128)(2,1)} %bitcast.121, bf16[64,4,4,128]{3,2,1,0:T(4,128)(2,1)} %slice.71, f32[4,4,64]{2,1,0:T(4,128)} %copy-done.14, f32[4,4,64]{2,1,0:T(4,128)S(1)} %get-tuple-element.13, f32[4,2048,64,4]{1,2,3,0:T(8,128)} %copy-done, ...), kind=kOutput, calls=%fused_computation.6 | convolution fusion | flops 551550976 | bytes 15085568 | tf_op jit(solution)/shard_map/tkgd,ckd->kgtc/dot_general | solution.py:76
  263.3 3.2 bitcast_multiply_fusion
  266.5 5.3 copy.53
  271.9 5.3 copy.57
  277.2 4.7 pad_add_fusion.1
  281.9 3.8 gather_fusion.2
  285.7 4.7 pad_add_fusion
  290.4 3.7 gather_fusion.3
  294.0 5.9 %select_convert_fusion = (bf16[32,64,512]{2,1,0:T(8,128)(2,1)}, bf16[32,64,512]{2,1,0:T(8,128)(2,1)}) fusion(bf16[32,64,512]{2,1,0:T(8,128)(2,1)} %gather_fusion.3, pred[32]{0:T(512)(128)(4,1)S(1)} %copy-done.15, bf16[32,64,512]{2,1,0:T(8,128)(2,1)} %gather_fusion.2), kind=kLoop, calls=%fused_computation.15 | loop fusion | flops 2097152 | bytes 8388640 | tf_op jit(solution)/shard_map/convert_element_type | solution.py:124
  308.2 131.1 %reduce-scatter.5.cloned.1.call-done = bf16[1,128,512]{2,1,0:T(8,128)(2,1)} async-done(((bf16[1,2048,512]{2,1,0:T(8,128)(2,1)}), bf16[1,128,512]{2,1,0:T(8,128)(2,1)}) %reduce-scatter.5.cloned.1.call-update) | async-done | bytes 131088 | tf_op jit(solution)/shard_map/reduce_scatter | solution.py:123
  440.9 95.1 %reduce-scatter.3.cloned.1.call-done = bf16[1,128,512]{2,1,0:T(8,128)(2,1)} async-done(((bf16[1,2048,512]{2,1,0:T(8,128)(2,1)}), bf16[1,128,512]{2,1,0:T(8,128)(2,1)}) %reduce-scatter.3.cloned.1.call-update) | async-done | bytes 131088 | tf_op jit(solution)/shard_map/reduce_scatter | solution.py:120
  537.7 4.7 convolution_convert_fusion
  (94 shorter events, 50.8 us)
Async XLA Ops:
  8.0 97.9 %all-gather.6.cloned.1.call-start = ((), (), s32[]{:S(2)}) async-start(), calls=%async_computation.3 | async-start | bytes 2228224 | tf_op jit(solution)/shard_map/all_gather | solution.py:44
  8.7 187.5 %all-gather.4.cloned.1.call-start = ((), (), s32[]{:S(2)}) async-start(), calls=%async_computation.2 | async-start | bytes 2228224 | tf_op jit(solution)/shard_map/all_gather | solution.py:43
  9.5 429.8 %reduce-scatter.5.cloned.1.call-start = ((), (), s32[]{:S(2)}) async-start(), calls=%async_computation.5 | async-start | bytes 2228224 | tf_op jit(solution)/shard_map/reduce_scatter | solution.py:123
  203.1 1.4 copy-start.4
  217.9 0.8 copy-start.12
  217.9 3.1 copy-start.11
  218.7 3.7 copy-start.3
  220.9 1.5 copy-start.9
  232.0 1.4 copy-start.5
  235.2 5.9 %copy-start.6 = (bf16[64,4,4,128]{3,2,1,0:T(4,128)(2,1)S(1)}, bf16[64,4,4,128]{3,2,1,0:T(4,128)(2,1)}, u32[]{:S(2)}) copy-start(bf16[64,4,4,128]{3,2,1,0:T(4,128)(2,1)} %slice.69) | copy-start | bytes 786436
  242.3 7.3 %copy-start = (f32[4,2048,64,4]{1,2,3,0:T(8,128)}, f32[4,2048,64,4]{1,2,3,0:T(8,128)S(1)}, u32[]{:S(2)}) copy-start(f32[4,2048,64,4]{1,2,3,0:T(8,128)S(1)} %fusion.15) | copy-start | bytes 25165828
  242.3 4.2 copy-start.7
  246.5 3.1 copy-start.14
  246.6 3.1 copy-start.8
  263.3 3.2 copy-start.1
  290.4 3.7 copy-start.15
  300.0 1.2 copy-start.13
  300.0 236.1 %reduce-scatter.3.cloned.1.call-start = ((), (), s32[]{:S(2)}) async-start(), calls=%async_computation.4 | async-start | bytes 2228224 | tf_op jit(solution)/shard_map/reduce_scatter | solution.py:120
  300.6 237.1 %all-gather.8.cloned.1.call-start = ((), (), s32[]{:S(2)}) async-start(), calls=%async_computation.6 | async-start | bytes 8650752 | tf_op jit(solution)/shard_map/all_gather | solution.py:134
  301.2 4.0 copy-start.2
  306.5 231.2 %copy-start.10 = (bf16[1,128,4096]{2,1,0:T(8,128)(2,1)S(1)}, bf16[1,128,4096]{2,1,0:T(8,128)(2,1)}, u32[]{:S(2)}) copy-start(bf16[1,128,4096]{2,1,0:T(8,128)(2,1)} %param.17) | copy-start | bytes 3145732
Sparse Core Ops, SparseCore 0:
  10.9 94.9 all-gather.5
  108.0 88.2 all-gather.3
  300.1 139.1 reduce-scatter.4
  442.0 94.0 reduce-scatter.2
Sparse Core Ops, SparseCore 1:
  304.4 116.3 all-gather.7
where the time goes:
time: 551 us; the launch traced here: 550 us
  waiting for transfers between devices  401 us (73%)
  local copies, waits for them, and re-layouts  58.1 us (11%)
  matrix products  38 us (7%)
  other arithmetic  35.6 us (6%)
  between operations  16.8 us (3%)
    reduce_scatter x1, waiting for transfers between devices, body(): lax.psum_scatter(value_terms.astype(jnp.bfloat16), 'ctx', scatter_dimensi...  131 us
    reduce_scatter x1, waiting for transfers between devices, body(): lax.psum_scatter(key_terms.astype(jnp.bfloat16), 'ctx', scatter_dimension...  95.1 us
    all_gather x1, waiting for transfers between devices, body(): lax.all_gather(k_pol, 'ctx', axis=1, tiled=True)  88 us
    all_gather x1, waiting for transfers between devices, body(): lax.all_gather(v_pol, 'ctx', axis=1, tiled=True)  84.8 us
    dot_general x2, matrix products, attend(): jnp.einsum('tkgd,ckd->kgtc', o_rows, v_part, preferred_element_type=jnp.f...  11.3 us
  transfers between devices with their start and end apart: 5, of which 4 were waited for; matrix products, arithmetic and copies ran while one was open for 4% of the time, Pallas kernels for 0%

commit v1 on v0

v1 whole, which is shorter than its diff:
```python
import functools
import jax
import jax.numpy as jnp
from jax import lax
from jax.experimental import pallas as pl
from jax.experimental.pallas import tpu as pltpu
from jax.sharding import PartitionSpec as P

MESH = pl.DeviceIdType.MESH
HD = 128
NX, NZ, NY = 4, 4, 8
GROUP = 4
ROWS = 128
HALF = 64
SCALE = HD ** -0.5
TK = 256
PAD = TK - HALF
NEG = -1e30
MIB = 1 << 20


def wrap(value, size):
    return lax.rem(value + size, size)


def place():
    wide = lax.axis_index("wide")
    ctx = lax.axis_index("ctx")
    return wide // 4, (wide // 2) % 2, wide % 2, ctx // NZ, ctx % NZ


def wide_id(y, zh, core):
    return (y * 2 + zh) * 2 + core


def ctx_peers(x, zl):
    peers = []
    for dz in (2, 1, 3, 0):
        for dx in (2, 1, 3, 0):
            if dz or dx:
                peers.append((wrap(x + dx, NX), wrap(zl + dz, NZ)))
    return peers


def meet(ids):
    barrier = pltpu.get_barrier_semaphore()
    for ident in ids:
        pl.semaphore_signal(barrier, inc=1, device_id=ident, device_id_type=MESH)
    pl.semaphore_wait(barrier, len(ids))


def remote(src, dst, sems, slot, ident):
    send, recv = sems
    return pltpu.make_async_remote_copy(
        src_ref=src, dst_ref=dst, send_sem=send.at[slot], recv_sem=recv.at[slot],
        device_id=ident, device_id_type=MESH,
    )


class WeightRing:
    def __init__(self, own, held, ring_sems, core_sems, core_dst=None):
        y, zh, core, x, zl = place()
        ctx = lax.axis_index("ctx")
        self.y, self.core = y, core
        self.own, self.held = own, held
        self.ring_sems, self.core_sems = ring_sems, core_sems
        self.right = (wide_id(wrap(y + 1, NY), zh, core), ctx)
        self.left = (wide_id(wrap(y - 1, NY), zh, core), ctx)
        self.other = (wide_id(y, zh, 1 - core), ctx)
        self.sent = []
        self.core_copies = []

    def chunk(self, owner, core, part):
        start = pl.multiple_of(core * ROWS + part * HALF, HALF)
        return self.held.at[owner, pl.ds(start, HALF)]

    def ring_copy(self, way, step, part):
        owner = wrap(self.y - (step - 1), NY) if way == 0 else wrap(self.y + (step - 1), NY)
        if step == 1:
            src = self.own.at[pl.ds(part * HALF, HALF)]
        else:
            src = self.chunk(owner, self.core, part)
        slot = (step - 1) * 4 + way * 2 + part
        return remote(src, self.chunk(owner, self.core, part), self.ring_sems, slot,
                      self.right if way == 0 else self.left)

    def arrival(self, way, step, part):
        owner = wrap(self.y - step, NY) if way == 0 else wrap(self.y + step, NY)
        dst = self.chunk(owner, self.core, part)
        slot = (step - 1) * 4 + way * 2 + part
        return remote(dst, dst, self.ring_sems, slot, self.right if way == 0 else self.left)

    def core_slot(self, way, step, part):
        return (step - 1) * 4 + way * 2 + part + 2

    def to_core(self, src, owner, part, slot):
        copy = remote(src, self.chunk(owner, self.core, part), self.core_sems, slot, self.other)
        copy.start()
        self.core_copies.append((copy, owner, part, slot))

    def valid(self, way, step, part):
        return step < 4 or (step == 4 and part == way)

    def begin(self):
        for part in range(2):
            for way in range(2):
                copy = self.ring_copy(way, 1, part)
                copy.start()
                self.sent.append(copy)
        for part in range(2):
            self.to_core(self.own.at[pl.ds(part * HALF, HALF)], self.y, part, part)

    def advance(self, step):
        for part in range(2):
            for way in range(2):
                if self.valid(way, step, part):
                    self.arrival(way, step, part).wait_recv()
                    if self.valid(way, step + 1, part):
                        copy = self.ring_copy(way, step + 1, part)
                        copy.start()
                        self.sent.append(copy)
                    owner = wrap(self.y - step, NY) if way == 0 else wrap(self.y + step, NY)
                    self.to_core(self.chunk(owner, self.core, part), owner, part, self.core_slot(way, step, part))

    def wait_core(self, copies):
        for copy, owner, part, slot in copies:
            dst = self.chunk(owner, 1 - self.core, part)
            remote(dst, dst, self.core_sems, slot, self.other).wait_recv()

    def finish_sends(self):
        for copy in self.sent:
            copy.wait_send()
        for copy, _, _, _ in self.core_copies:
            copy.wait_send()


def gather_kernel(q, k, v, do, w, q_in, do_in, kv_in, held, other_w,
                  x_send, x_recv, kv_send, kv_recv, ring_send, ring_recv, core_send, core_recv, zh_send, zh_recv,
                  local_sem):
    y, zh, core, x, zl = place()
    wide = lax.axis_index("wide")
    ctx = lax.axis_index("ctx")
    ring = WeightRing(w, held, (ring_send, ring_recv), (core_send, core_recv))
    across = (wide_id(y, 1 - zh, core), x * NZ + (NZ - 1 - zl))
    inner = (wide, x * NZ + 1 + zl // 3)
    edge = (zl == 0) | (zl == NZ - 1)
    peers = ctx_peers(x, zl)
    meet([(wide, px * NZ + pz) for px, pz in peers] + [ring.right, ring.left, ring.other, across])

    to_across = remote(w, other_w, (zh_send, zh_recv), 0, across)
    to_inner = remote(other_w, other_w, (zh_send, zh_recv), 1, inner)
    pl.when(edge)(to_across.start)
    ring.begin()

    def cols(index, width):
        return pl.ds(pl.multiple_of(index * width, width), width)

    copies = []
    for n, (px, pz) in enumerate(peers):
        for j, src in enumerate((k, v)):
            copy = remote(src.at[0, :, cols(px, HD)], kv_in.at[ctx, j], (kv_send, kv_recv), 2 * n + j, (wide, px * NZ + pz))
            copy.start()
            copies.append(copy)
    for n, dx in enumerate((2, 1, 3)):
        px = wrap(x + dx, NX)
        for j, (src, dst) in enumerate(((q, q_in), (do, do_in))):
            copy = remote(src.at[0, :, cols(px, GROUP * HD)], dst.at[x], (x_send, x_recv), 2 * n + j, (wide, px * NZ + zl))
            copy.start()
            copies.append(copy)
    local = [
        pltpu.make_async_copy(q.at[0, :, cols(x, GROUP * HD)], q_in.at[x], local_sem.at[0]),
        pltpu.make_async_copy(do.at[0, :, cols(x, GROUP * HD)], do_in.at[x], local_sem.at[1]),
        pltpu.make_async_copy(k.at[0, :, cols(x, HD)], kv_in.at[ctx, 0], local_sem.at[2]),
        pltpu.make_async_copy(v.at[0, :, cols(x, HD)], kv_in.at[ctx, 1], local_sem.at[3]),
        pltpu.make_async_copy(w, held.at[y, pl.ds(pl.multiple_of(core * ROWS, ROWS), ROWS)], local_sem.at[4]),
    ]
    for copy in local:
        copy.start()

    @pl.when(edge)
    def _():
        to_across.wait_recv()
        to_inner.start()

    for step in range(1, 5):
        ring.advance(step)

    @pl.when(edge)
    def _():
        to_across.wait_send()
        to_inner.wait_send()

    @pl.when(jnp.logical_not(edge))
    def _():
        to_inner.wait_recv()

    for copy in copies:
        copy.wait()
    ring.wait_core(ring.core_copies)
    ring.finish_sends()
    for copy in local:
        copy.wait()


def attend_kernel(map_ref, len_ref, q_in, do_in, kv_in, dq_out, terms, kpos, vpos, dkpos, dvpos, s_ref, g_ref):
    zl = lax.axis_index("ctx") % NZ
    kpos[pl.ds(0, PAD)] = jnp.zeros((PAD, HD), jnp.bfloat16)
    vpos[pl.ds(0, PAD)] = jnp.zeros((PAD, HD), jnp.bfloat16)
    dkpos[...] = jnp.zeros_like(dkpos)
    dvpos[...] = jnp.zeros_like(dvpos)

    def place_block(i, carry):
        for j in range(2):
            at = pl.ds(pl.multiple_of(map_ref[i, j] * HALF + PAD, HALF), HALF)
            kpos[at] = kv_in[i, 0, pl.ds(j * HALF, HALF)]
            vpos[at] = kv_in[i, 1, pl.ds(j * HALF, HALF)]
        return carry

    lax.fori_loop(0, NX * NZ, place_block, 0)
    end0 = len_ref[0, 0]
    end1 = end0 + len_ref[0, 1]
    end2 = end1 + len_ref[0, 2]
    end3 = end2 + len_ref[0, 3]

    def doc_start(pos):
        start = jnp.zeros_like(pos)
        for end in (end0, end1, end2, end3):
            start = jnp.where(pos >= end, end, start)
        return start

    def nt(a, b):
        return lax.dot_general(a, b, (((1,), (1,)), ((), ())), preferred_element_type=jnp.float32)

    def tn(a, b):
        return lax.dot_general(a, b, (((0,), (0,)), ((), ())), preferred_element_type=jnp.float32)

    def row_block(n, carry):
        xs, j = n // 2, n % 2
        block = map_ref[xs * NZ + zl, j]
        base = block * HALF
        start = doc_start(base)
        span = base + HALF - (start // HALF) * HALF
        tiles = (span + TK - 1) // TK
        rows = pl.ds(pl.multiple_of(j * HALF, HALF), HALF)
        q = jnp.concatenate([q_in[xs, rows, h * HD:(h + 1) * HD] for h in range(GROUP)], axis=0)
        do = jnp.concatenate([do_in[xs, rows, h * HD:(h + 1) * HD] for h in range(GROUP)], axis=0)
        pos = base + lax.broadcasted_iota(jnp.int32, (HALF, 1), 0)
        first = doc_start(pos)

        def scores(t, top):
            at = pl.ds(pl.multiple_of(base - t * TK, HALF), TK)
            kp = base - t * TK - PAD + lax.broadcasted_iota(jnp.int32, (HALF, TK), 1)
            bias = jnp.where((kp <= pos) & (kp >= first), 0.0, NEG)
            s = nt(q, kpos[at]) * SCALE
            s = (s.reshape(GROUP, HALF, TK) + bias[None]).reshape(GROUP * HALF, TK)
            s_ref[t] = s
            g_ref[t] = nt(do, vpos[at])
            for c in range(TK // 128):
                top = jnp.maximum(top, s[:, c * 128:(c + 1) * 128])
            return top

        top = lax.fori_loop(0, tiles, scores, jnp.full((GROUP * HALF, 128), NEG, jnp.float32))
        top = jnp.max(top, axis=1, keepdims=True)

        def weigh(t, sums):
            total, delta = sums
            p = jnp.exp(s_ref[t] - top)
            s_ref[t] = p
            pg = p * g_ref[t]
            for c in range(TK // 128):
                total = total + p[:, c * 128:(c + 1) * 128]
                delta = delta + pg[:, c * 128:(c + 1) * 128]
            return total, delta

        zero = jnp.zeros((GROUP * HALF, 128), jnp.float32)
        total, delta = lax.fori_loop(0, tiles, weigh, (zero, zero))
        inverse = 1.0 / jnp.sum(total, axis=1, keepdims=True)
        delta = jnp.sum(delta, axis=1, keepdims=True) * inverse

        def grads(t, dq):
            at = pl.ds(pl.multiple_of(base - t * TK, HALF), TK)
            p = s_ref[t] * inverse
            ds = (p * (g_ref[t] - delta)).astype(jnp.bfloat16)
            dkpos[at] += tn(ds, q)
            dvpos[at] += tn(p.astype(jnp.bfloat16), do)
            return dq + jnp.dot(ds, kpos[at], preferred_element_type=jnp.float32)

        dq = lax.fori_loop(0, tiles, grads, jnp.zeros((GROUP * HALF, HD), jnp.float32))
        dq = (dq * SCALE).astype(jnp.bfloat16)
        for h in range(GROUP):
            dq_out[xs, rows, h * HD:(h + 1) * HD] = dq[h * HALF:(h + 1) * HALF]
        return carry

    lax.fori_loop(0, 2 * NX, row_block, 0)

    def store_block(i, carry):
        for j in range(2):
            at = pl.ds(pl.multiple_of(map_ref[i, j] * HALF + PAD, HALF), HALF)
            terms[i, 0, pl.ds(j * HALF, HALF)] = (dkpos[at] * SCALE).astype(jnp.bfloat16)
            terms[i, 1, pl.ds(j * HALF, HALF)] = dvpos[at].astype(jnp.bfloat16)
        return carry

    lax.fori_loop(0, NX * NZ, store_block, 0)


def return_kernel(dq_out, terms, held, other_w, h, gain, dq, dk, dv, kref, vref,
                  dq_got, terms_got, own_v, far_v, h_v, normed, acc,
                  x_send, x_recv, t_send, t_recv, ring_send, ring_recv, core_send, core_recv, local_sem):
    y, zh, core, x, zl = place()
    wide = lax.axis_index("wide")
    ctx = lax.axis_index("ctx")
    ring = WeightRing(other_w, far_v, (ring_send, ring_recv), (core_send, core_recv))
    load_h = pltpu.make_async_copy(h.at[0], h_v, local_sem.at[0])
    load_w = pltpu.make_async_copy(held, own_v, local_sem.at[1])
    load_h.start()
    load_w.start()
    peers = ctx_peers(x, zl)
    meet([(wide, px * NZ + pz) for px, pz in peers] + [ring.right, ring.left, ring.other])

    ring.begin()
    copies = []
    for n, (px, pz) in enumerate(peers):
        copy = remote(terms.at[px * NZ + pz], terms_got.at[ctx], (t_send, t_recv), n, (wide, px * NZ + pz))
        copy.start()
        copies.append(copy)
    for n, dx in enumerate((2, 1, 3)):
        px = wrap(x + dx, NX)
        copy = remote(dq_out.at[px], dq_got.at[x], (x_send, x_recv), n, (wide, px * NZ + zl))
        copy.start()
        copies.append(copy)
    local = [
        pltpu.make_async_copy(dq_out.at[x], dq_got.at[x], local_sem.at[2]),
        pltpu.make_async_copy(terms.at[ctx], terms_got.at[ctx], local_sem.at[3]),
        pltpu.make_async_copy(other_w, far_v.at[y, pl.ds(pl.multiple_of(core * ROWS, ROWS), ROWS)], local_sem.at[4]),
    ]
    for copy in local:
        copy.start()

    load_h.wait()
    strip = 16

    def norm_rows(i, carry):
        rows = pl.ds(pl.multiple_of(i * strip, strip), strip)
        a = h_v[rows].astype(jnp.float32)
        mean = jnp.mean(a * a, axis=1, keepdims=True)
        normed[rows] = (a * lax.rsqrt(mean + 1e-05) * gain[...].astype(jnp.float32)).astype(jnp.bfloat16)
        return carry

    lax.fori_loop(0, ROWS // strip, norm_rows, 0)
    load_w.wait()
    acc[...] = jnp.zeros_like(acc)

    def project(weights, zh_of, owner):
        at = pl.ds(pl.multiple_of((2 * owner + zh_of) * 2 * ROWS, 2 * ROWS), 2 * ROWS)
        acc[...] += jnp.dot(normed[:, at], weights[owner], preferred_element_type=jnp.float32)

    def near(i, carry):
        project(own_v, zh, i)
        return carry

    lax.fori_loop(0, 4, near, 0)
    ring.advance(1)
    lax.fori_loop(4, 8, near, 0)
    ring.advance(2)
    ring.advance(3)
    ring.advance(4)
    ring.wait_core(ring.core_copies)
    for copy in local:
        copy.wait()

    def far(i, carry):
        project(far_v, 1 - zh, i)
        return carry

    lax.fori_loop(0, NY, far, 0)
    kref[0] = acc[:, :512].astype(jnp.bfloat16)
    vref[0] = acc[:, 512:].astype(jnp.bfloat16)
    for copy in copies:
        copy.wait()
    ring.finish_sends()
    for xs in range(NX):
        dq[0, :, xs * 512:(xs + 1) * 512] = dq_got[xs].astype(jnp.float32)
        for j, out in enumerate((dk, dv)):
            total = terms_got[xs * NZ, j].astype(jnp.float32)
            for zs in range(1, NZ):
                total = total + terms_got[xs * NZ + zs, j].astype(jnp.float32)
            out[0, :, xs * HD:(xs + 1) * HD] = total


def body(q_pol, k_pol, v_pol, d_out, h_ref, norm_gain, w_kv_ref, lengths, block_map):
    bf16, f32 = jnp.bfloat16, jnp.float32
    any_spec = pl.BlockSpec(memory_space=pl.ANY)
    vmem = pl.BlockSpec(memory_space=pltpu.VMEM)
    smem = pl.BlockSpec(memory_space=pltpu.SMEM)
    dma = pltpu.SemaphoreType.DMA
    shape = jax.ShapeDtypeStruct
    q_in, do_in, kv_in, held, other_w = pl.pallas_call(
        gather_kernel,
        name="gather_inputs",
        out_shape=(
            shape((NX, ROWS, GROUP * HD), bf16),
            shape((NX, ROWS, GROUP * HD), bf16),
            shape((NX * NZ, 2, ROWS, HD), bf16),
            shape((NY, 2 * ROWS, 1024), bf16),
            shape((ROWS, 1024), bf16),
        ),
        in_specs=[any_spec] * 5,
        out_specs=(any_spec,) * 5,
        scratch_shapes=[
            dma((6,)), dma((6,)), dma((30,)), dma((30,)), dma((16,)), dma((16,)), dma((18,)), dma((18,)),
            dma((2,)), dma((2,)), dma((5,)),
        ],
        compiler_params=pltpu.CompilerParams(collective_id=0, has_side_effects=True),
    )(q_pol, k_pol, v_pol, d_out, w_kv_ref)
    dq_out, terms = pl.pallas_call(
        attend_kernel,
        name="attend",
        out_shape=(shape((NX, ROWS, GROUP * HD), bf16), shape((NX * NZ, 2, ROWS, HD), bf16)),
        in_specs=[smem, smem, vmem, vmem, vmem],
        out_specs=(vmem, vmem),
        scratch_shapes=[
            pltpu.VMEM((PAD + 2048, HD), bf16),
            pltpu.VMEM((PAD + 2048, HD), bf16),
            pltpu.VMEM((PAD + 2048, HD), f32),
            pltpu.VMEM((PAD + 2048, HD), f32),
            pltpu.VMEM((5, GROUP * HALF, TK), f32),
            pltpu.VMEM((5, GROUP * HALF, TK), f32),
        ],
        compiler_params=pltpu.CompilerParams(vmem_limit_bytes=32 * MIB),
    )(block_map, lengths, q_in, do_in, kv_in)
    return pl.pallas_call(
        return_kernel,
        name="return_results",
        out_shape=(
            shape((1, ROWS, 2048), f32),
            shape((1, ROWS, 512), f32),
            shape((1, ROWS, 512), f32),
            shape((1, ROWS, 512), bf16),
            shape((1, ROWS, 512), bf16),
        ),
        in_specs=[any_spec] * 5 + [vmem],
        out_specs=(vmem,) * 5,
        scratch_shapes=[
            pltpu.VMEM((NX, ROWS, GROUP * HD), bf16),
            pltpu.VMEM((NX * NZ, 2, ROWS, HD), bf16),
            pltpu.VMEM((NY, 2 * ROWS, 1024), bf16),
            pltpu.VMEM((NY, 2 * ROWS, 1024), bf16),
            pltpu.VMEM((ROWS, 4096), bf16),
            pltpu.VMEM((ROWS, 4096), bf16),
            pltpu.VMEM((ROWS, 1024), f32),
            dma((3,)), dma((3,)), dma((15,)), dma((15,)), dma((16,)), dma((16,)), dma((18,)), dma((18,)), dma((5,)),
        ],
        compiler_params=pltpu.CompilerParams(
            collective_id=1, has_side_effects=True, vmem_limit_bytes=48 * MIB
        ),
    )(dq_out, terms, held, other_w, h_ref, norm_gain.reshape(1, -1))


def solution(mesh):
    rows = P("wide", "ctx", None)
    return jax.shard_map(
        body,
        mesh=mesh,
        in_specs=(rows, rows, rows, rows, rows, P(), P("wide", None), P("wide", None), P()),
        out_specs=(rows,) * 5,
        check_vma=False,
    )
```

time: 551 us -> 105 us (0.19)
  the two profiles are of different devices: /device:TPU:16 before, /device:TPU:1 now
where the time goes in v1:
time: 105 us
  Pallas kernels  94.1 us (90%)
  local copies, waits for them, and re-layouts  10.1 us (10%)
    pallas_call x1, Pallas kernels, body(): pl.pallas_call(gather_kernel, name='gather_inputs', out_shape=(shape((NX,...  43.3 us
    pallas_call x1, Pallas kernels, body(): pl.pallas_call(return_kernel, name='return_results', out_shape=(shape((1,...  36.8 us
    pallas_call x1, Pallas kernels, body(): pl.pallas_call(attend_kernel, name='attend', out_shape=(shape((NX, ROWS,...  13.9 us
    unnamed x18, local copies, waits for them, and re-layouts  9.35 us

profile of v1, /device:TPU:1, one launch (start us, length us, event | category | flops | bytes accessed | tf_op | source)
XLA Modules:
  0.0 104.9 jit_solution(810931342029534765)
XLA Ops:
  0.6 0.0 copy-start
  0.6 43.3 %gather_inputs.1 = (bf16[4,128,512]{2,1,0:T(8,128)(2,1)}, bf16[4,128,512]{2,1,0:T(8,128)(2,1)}, bf16[16,2,128,128]{3,2,1,0:T(8,128)(2,1)}, bf16[8,256,1024]{2,1,0:T(8,128)(2,1)}, bf16[128,1024]{1,0:T(8,128)(2,1)}) custom-call(bf16[1,128,2048]{2,1,0:T(8,128)(2,1)} %q.1, bf16[1,128,512]{2,1,0:T(8,128)(2,1)} %k.1, bf16[1,128,512]{2,1,0:T(8,128)(2,1)} %v.1, ...), custom_call_target="tpu_custom_call" | custom-call | tf_op jit(solution)/shard_map/gather_inputs/pallas_call | solution.py:397
  44.0 0.8 copy.14.map_ref
  44.7 0.0 copy-start.1
  44.7 1.2 %copy-done.1 = bf16[16,2,128,128]{3,2,1,0:T(8,128)(2,1)S(1)} copy-done((bf16[16,2,128,128]{3,2,1,0:T(8,128)(2,1)S(1)}, bf16[16,2,128,128]{3,2,1,0:T(8,128)(2,1)}, u32[]{:S(2)}) %copy-start.1) | copy-done | bytes 1048600
  46.0 0.0 copy-start.2
  46.0 1.0 copy-done.2
  47.0 0.0 copy-start.3
  47.0 1.0 copy-done.3
  48.0 0.0 copy-start.5
  48.0 0.7 copy-done.5
  48.7 13.9 %attend.1 = (bf16[4,128,512]{2,1,0:T(8,128)(2,1)S(1)}, bf16[16,2,128,128]{3,2,1,0:T(8,128)(2,1)S(1)}) custom-call(s32[16,2]{1,0:T(8,128)S(1)} %copy.14.map_ref, s32[1,4]{1,0:T(1,128)S(1)} %copy-done.5, bf16[4,128,512]{2,1,0:T(8,128)(2,1)S(1)} %copy-done.2, bf16[4,128,512]{2,1,0:T(8,128)(2,1)S(1)} %copy-done.3, bf16[16,2,128,128]{3,2,1,0:T(8,128)(2,1)S(1)} %copy-done.1), custom_call_target="tpu_custom_call" | custom-call | tf_op jit(solution)/shard_map/attend/pallas_call | solution.py:415
  62.7 0.7 reshape.13.gain
  63.4 0.0 copy-done
  63.4 0.0 copy-start.4
  63.4 0.9 copy-done.4
  64.3 36.8 %return_results.1 = (f32[1,128,2048]{2,1,0:T(8,128)S(1)}, f32[1,128,512]{2,1,0:T(8,128)S(1)}, f32[1,128,512]{2,1,0:T(8,128)S(1)}, bf16[1,128,512]{2,1,0:T(8,128)(2,1)S(1)}, bf16[1,128,512]{2,1,0:T(8,128)(2,1)S(1)}) custom-call(bf16[4,128,512]{2,1,0:T(8,128)(2,1)S(1)} %get-tuple-element.15.dq_out, bf16[16,2,128,128]{3,2,1,0:T(8,128)(2,1)S(1)} %get-tuple-element.16.terms, ...), custom_call_target="tpu_custom_call" | custom-call | tf_op jit(solution)/shard_map/return_results/pallas_call | solution.py:431
  101.2 1.0 copy.20
  102.2 0.7 copy.21
  102.9 0.7 copy.22
  103.6 0.7 copy.23
  104.2 0.7 copy.24
Async XLA Ops:
  0.6 62.7 %copy-start = (bf16[1,128,4096]{2,1,0:T(8,128)(2,1)S(1)}, bf16[1,128,4096]{2,1,0:T(8,128)(2,1)}, u32[]{:S(2)}) copy-start(bf16[1,128,4096]{2,1,0:T(8,128)(2,1)} %h.1) | copy-start | bytes 3145732
  44.7 1.2 %copy-start.1 = (bf16[16,2,128,128]{3,2,1,0:T(8,128)(2,1)S(1)}, bf16[16,2,128,128]{3,2,1,0:T(8,128)(2,1)}, u32[]{:S(2)}) copy-start(bf16[16,2,128,128]{3,2,1,0:T(8,128)(2,1)} %get-tuple-element.14.kv_in) | copy-start | bytes 3145732
  46.0 1.0 copy-start.2
  47.0 1.0 copy-start.3
  48.0 0.7 copy-start.5
  63.4 1.0 copy-start.4

commit v2 on v1

v2 whole, which is shorter than its diff:
```python
import functools
import jax
import jax.numpy as jnp
from jax import lax
from jax.experimental import pallas as pl
from jax.experimental.pallas import tpu as pltpu
from jax.sharding import PartitionSpec as P

MESH = pl.DeviceIdType.MESH
HD = 128
NX, NZ, NY = 4, 4, 8
GROUP = 4
ROWS = 128
HALF = 64
SCALE = HD ** -0.5
TK = 256
WINDOW = 1024 + HALF
BACK = WINDOW // HALF - 1
TILES = tuple((off, min(TK, WINDOW - off)) for off in range(0, WINDOW, TK))
NEG = -1e30
LOG2E = 1.4426950408889634
MIB = 1 << 20
VMEM_ALL = 63 * MIB


def wrap(value, size):
    return lax.rem(value + size, size)


def place():
    wide = lax.axis_index("wide")
    ctx = lax.axis_index("ctx")
    return wide // 4, (wide // 2) % 2, wide % 2, ctx // NZ, ctx % NZ


def wide_id(y, zh, core):
    return (y * 2 + zh) * 2 + core


def ctx_peers(x, zl):
    peers = []
    for dz in (2, 1, 3, 0):
        for dx in (2, 1, 3, 0):
            if dz or dx:
                peers.append((wrap(x + dx, NX), wrap(zl + dz, NZ)))
    return peers


def meet(ids):
    barrier = pltpu.get_barrier_semaphore()
    for ident in ids:
        pl.semaphore_signal(barrier, inc=1, device_id=ident, device_id_type=MESH)
    pl.semaphore_wait(barrier, len(ids))


def remote(src, dst, sems, slot, ident):
    send, recv = sems
    return pltpu.make_async_remote_copy(
        src_ref=src, dst_ref=dst, send_sem=send.at[slot], recv_sem=recv.at[slot],
        device_id=ident, device_id_type=MESH,
    )


class WeightRing:
    def __init__(self, own, held, ring_sems, core_sems, core_dst=None):
        y, zh, core, x, zl = place()
        ctx = lax.axis_index("ctx")
        self.y, self.core = y, core
        self.own, self.held = own, held
        self.ring_sems, self.core_sems = ring_sems, core_sems
        self.right = (wide_id(wrap(y + 1, NY), zh, core), ctx)
        self.left = (wide_id(wrap(y - 1, NY), zh, core), ctx)
        self.other = (wide_id(y, zh, 1 - core), ctx)
        self.sent = []
        self.core_copies = []

    def chunk(self, owner, core, part):
        start = pl.multiple_of(core * ROWS + part * HALF, HALF)
        return self.held.at[owner, pl.ds(start, HALF)]

    def ring_copy(self, way, step, part):
        owner = wrap(self.y - (step - 1), NY) if way == 0 else wrap(self.y + (step - 1), NY)
        if step == 1:
            src = self.own.at[pl.ds(part * HALF, HALF)]
        else:
            src = self.chunk(owner, self.core, part)
        slot = (step - 1) * 4 + way * 2 + part
        return remote(src, self.chunk(owner, self.core, part), self.ring_sems, slot,
                      self.right if way == 0 else self.left)

    def arrival(self, way, step, part):
        owner = wrap(self.y - step, NY) if way == 0 else wrap(self.y + step, NY)
        dst = self.chunk(owner, self.core, part)
        slot = (step - 1) * 4 + way * 2 + part
        return remote(dst, dst, self.ring_sems, slot, self.right if way == 0 else self.left)

    def core_slot(self, way, step, part):
        return (step - 1) * 4 + way * 2 + part + 2

    def to_core(self, src, owner, part, slot):
        copy = remote(src, self.chunk(owner, self.core, part), self.core_sems, slot, self.other)
        copy.start()
        self.core_copies.append((copy, owner, part, slot))

    def valid(self, way, step, part):
        return step < 4 or (step == 4 and part == way)

    def begin(self):
        for way in range(2):
            copy = self.ring_copy(way, 1, 0)
            copy.start()
            self.sent.append(copy)
        for part in range(2):
            self.to_core(self.own.at[pl.ds(part * HALF, HALF)], self.y, part, part)

    def begin_second(self):
        for copy in self.sent[:2]:
            copy.wait_send()
        for way in range(2):
            copy = self.ring_copy(way, 1, 1)
            copy.start()
            self.sent.append(copy)

    def advance(self, step):
        for part in range(2):
            for way in range(2):
                if self.valid(way, step, part):
                    self.arrival(way, step, part).wait_recv()
                    if self.valid(way, step + 1, part):
                        copy = self.ring_copy(way, step + 1, part)
                        copy.start()
                        self.sent.append(copy)
                    owner = wrap(self.y - step, NY) if way == 0 else wrap(self.y + step, NY)
                    self.to_core(self.chunk(owner, self.core, part), owner, part, self.core_slot(way, step, part))

    def wait_core(self, copies):
        for copy, owner, part, slot in copies:
            dst = self.chunk(owner, 1 - self.core, part)
            remote(dst, dst, self.core_sems, slot, self.other).wait_recv()

    def finish_sends(self):
        for copy in self.sent[2:]:
            copy.wait_send()
        for copy, _, _, _ in self.core_copies:
            copy.wait_send()


class Line:
    def __init__(self, zl):
        half = zl // 2
        self.partner = zl + 1 - 2 * (zl % 2)
        self.far_inner = 2 - half
        self.far_edge = 3 - 3 * half
        self.edge = (zl == 0) | (zl == NZ - 1)
        self.inner = (zl == 1) | (zl == 2)


def cols(index, width):
    return pl.ds(pl.multiple_of(index * width, width), width)


def dot_nt(a, b):
    return lax.dot_general(a, b, (((1,), (1,)), ((), ())), preferred_element_type=jnp.float32)


def dot_tn(a, b):
    return lax.dot_general(a, b, (((0,), (0,)), ((), ())), preferred_element_type=jnp.float32)


def fold(values, combine):
    parts = [values[i:i + 8] for i in range(0, values.shape[0], 8)]
    while len(parts) > 1:
        parts = [combine(parts[i], parts[i + 1]) if i + 1 < len(parts) else parts[i] for i in range(0, len(parts), 2)]
    return parts[0]


def step_kernel(map_ref, len_ref, q, k, v, do, w, h, gain, dq_got, terms_got, projected,
                q_v, do_v, kv_v, kpos, vpos, s_ref, g_ref, dkw, dvw, terms_v, dq_v, passed,
                near_v, far_v, h_v, normed, acc,
                x_send, x_recv, kx_send, kx_recv, kz_send, kz_recv, relay_send, zh_send, zh_recv,
                dq_send, dq_recv, t_send, t_recv, pass_send, pass_recv, sum_send, sum_recv,
                near_send, near_recv, near_csend, near_crecv, far_send, far_recv, far_csend, far_crecv, local_sem):
    y, zh, core, x, zl = place()
    wide = lax.axis_index("wide")
    line = Line(zl)
    own_rows = pl.ds(pl.multiple_of(core * ROWS, ROWS), ROWS)
    own_slot = zl * NX + x
    loads = [
        pltpu.make_async_copy(k.at[0, :, cols(x, HD)], kv_v.at[own_slot, 0], local_sem.at[0]),
        pltpu.make_async_copy(v.at[0, :, cols(x, HD)], kv_v.at[own_slot, 1], local_sem.at[1]),
        pltpu.make_async_copy(h.at[0], h_v, local_sem.at[2]),
        pltpu.make_async_copy(q.at[0, :, cols(x, GROUP * HD)], q_v.at[x], local_sem.at[3]),
        pltpu.make_async_copy(do.at[0, :, cols(x, GROUP * HD)], do_v.at[x], local_sem.at[4]),
        pltpu.make_async_copy(w, near_v.at[y, own_rows], local_sem.at[5]),
    ]
    for copy in loads:
        copy.start()
    near = WeightRing(w, near_v, (near_send, near_recv), (near_csend, near_crecv))
    far_own = far_v.at[y, own_rows]
    far = WeightRing(far_own, far_v, (far_send, far_recv), (far_csend, far_crecv))
    across = (wide_id(y, 1 - zh, core), x * NZ + (NZ - 1 - zl))
    partner = (wide, x * NZ + line.partner)
    far_inner = (wide, x * NZ + line.far_inner)
    far_z = (line.far_inner, line.far_edge)
    meet([(wide, px * NZ + pz) for px, pz in ctx_peers(x, zl)] + [near.right, near.left, near.other, across])

    kx = {}
    for d in (1, 3, 2):
        px = wrap(x + d, NX)
        for j, src in enumerate((k, v)):
            kx[d, j] = remote(src.at[0, :, cols(px, HD)], kv_v.at[own_slot, j], (kx_send, kx_recv), 2 * (d - 1) + j,
                              (wide, px * NZ + zl))
            kx[d, j].start()
    to_across = remote(w, far_own, (zh_send, zh_recv), 0, across)
    to_inner = remote(far_own, far_own, (zh_send, zh_recv), 1, partner)
    pl.when(line.edge)(to_across.start)
    near.begin()

    def piece(z, d, send_sem, ident):
        slot = z * NX + wrap(x + d, NX)
        return pltpu.make_async_remote_copy(
            src_ref=kv_v.at[slot], dst_ref=kv_v.at[slot], send_sem=send_sem, recv_sem=kz_recv.at[slot],
            device_id=ident, device_id_type=MESH,
        )

    kz = []

    def along(d):
        for n, ident in enumerate((far_inner, partner)):
            copy = piece(zl, d, kz_send.at[2 * d + n], ident)
            copy.start()
            kz.append(copy)

    def arrived(z, d):
        piece(z, d, kz_send.at[0], partner).wait_recv()

    def relay_copy(n, d):
        return piece(far_z[n], d, relay_send.at[2 * d + n], partner)

    def relay(d):
        @pl.when(line.inner)
        def _():
            for n in range(2):
                arrived(far_z[n], d)
                relay_copy(n, d).start()

    loads[0].wait()
    loads[1].wait()
    along(0)
    for d in (1, 3, 2):
        for j in range(2):
            kx[d, j].wait_recv()
        along(NX - d)
    qd = {}
    for d in (1, 3, 2):
        px = wrap(x + d, NX)
        for j, (src, dst) in enumerate(((q, q_v), (do, do_v))):
            qd[d, j] = remote(src.at[0, :, cols(px, GROUP * HD)], dst.at[x], (x_send, x_recv), 2 * (d - 1) + j,
                              (wide, px * NZ + zl))
            qd[d, j].start()
    relay(0)
    near.begin_second()

    kpos[pl.ds(0, BACK)] = jnp.zeros((BACK, HALF, HD), jnp.bfloat16)
    vpos[pl.ds(0, BACK)] = jnp.zeros((BACK, HALF, HD), jnp.bfloat16)
    relay(3)
    near.advance(1)

    @pl.when(line.edge)
    def _():
        to_across.wait_recv()
        to_inner.start()

    relay(1)
    loads[2].wait()
    strip = 16

    def norm_rows(i, carry):
        rows = pl.ds(pl.multiple_of(i * strip, strip), strip)
        a = h_v[rows].astype(jnp.float32)
        mean = jnp.mean(a * a, axis=1, keepdims=True)
        normed[rows] = (a * lax.rsqrt(mean + 1e-05) * gain[...].astype(jnp.float32)).astype(jnp.bfloat16)
        return carry

    lax.fori_loop(0, ROWS // strip, norm_rows, 0)
    acc[...] = jnp.zeros_like(acc)
    near.advance(2)
    relay(2)

    def project(weights, zh_of, owner):
        at = pl.ds(pl.multiple_of((2 * owner + zh_of) * 2 * ROWS, 2 * ROWS), 2 * ROWS)
        acc[...] += jnp.dot(normed[:, at], weights[owner], preferred_element_type=jnp.float32)

    def project_near(i, carry):
        project(near_v, zh, wrap(y + i - 2 + NY, NY))
        return carry

    def project_far(i, carry):
        project(far_v, 1 - zh, wrap(y + i - 2 + NY, NY))
        return carry

    @pl.when(line.edge)
    def _():
        for d in (0, 3, 1, 2):
            for n in range(2):
                arrived(far_z[n], d)

    for d in range(NX):
        arrived(line.partner, d)

    def place_block(p, carry):
        slot = jnp.int32(0)
        for i in range(NX * NZ):
            slot = jnp.where(map_ref[0, i] == p, (i % NZ) * NX + i // NZ, slot)
        for j, dst in enumerate((kpos, vpos)):
            pair = kv_v[slot, j]
            dst[BACK + p] = pair[:HALF]
            dst[BACK + 2 * NX * NZ - 1 - p] = pair[HALF:]
        return carry

    lax.fori_loop(0, NX * NZ, place_block, 0)
    ends = [len_ref[0, 0]]
    for i in range(1, 4):
        ends.append(ends[-1] + len_ref[0, i])

    def doc_start(pos):
        start = jnp.zeros_like(pos)
        for end in ends:
            start = jnp.where(pos >= end, end, start)
        return start

    def row_block(d, j):
        xs = wrap(x + d, NX)
        n = 2 * d + j
        block = map_ref[j, xs * NZ + zl]
        base = block * HALF
        rows = pl.ds(pl.multiple_of(j * HALF, HALF), HALF)
        qb = jnp.concatenate([q_v[xs, rows, i * HD:(i + 1) * HD] for i in range(GROUP)], axis=0)
        dob = jnp.concatenate([do_v[xs, rows, i * HD:(i + 1) * HD] for i in range(GROUP)], axis=0)
        lane = lax.broadcasted_iota(jnp.int32, (1, GROUP * HALF), 1)
        pos = base + lane % HALF
        first = doc_start(pos)
        top = jnp.full((8, GROUP * HALF), NEG, jnp.float32)

        def tile(ref, off, size):
            first_block = block + (WINDOW - off - size) // HALF
            parts = [ref[first_block + i] for i in range(size // HALF)]
            return jnp.concatenate(parts, axis=0) if len(parts) > 1 else parts[0]

        for off, size in TILES:
            kp = base + HALF - off - size + lax.broadcasted_iota(jnp.int32, (size, GROUP * HALF), 0)
            s = jnp.where((kp <= pos) & (kp >= first), dot_nt(tile(kpos, off, size), qb), NEG)
            s_ref[off:off + size] = s
            g_ref[off:off + size] = dot_nt(tile(vpos, off, size), dob)
            top = jnp.maximum(top, fold(s, jnp.maximum))
        top = jnp.max(top, axis=0, keepdims=True)
        total = jnp.zeros((8, GROUP * HALF), jnp.float32)
        delta = jnp.zeros((8, GROUP * HALF), jnp.float32)
        for off, size in TILES:
            p = jnp.exp2((s_ref[off:off + size] - top) * (SCALE * LOG2E))
            s_ref[off:off + size] = p
            total = total + fold(p, jnp.add)
            delta = delta + fold(p * g_ref[off:off + size], jnp.add)
        inverse = 1.0 / jnp.sum(total, axis=0, keepdims=True)
        delta = jnp.sum(delta, axis=0, keepdims=True) * inverse
        dq = jnp.zeros((HD, GROUP * HALF), jnp.float32)
        for off, size in TILES:
            p = s_ref[off:off + size] * inverse
            ds = (p * (g_ref[off:off + size] - delta)).astype(jnp.bfloat16)
            to = pl.ds((WINDOW - off - size) // HALF, size // HALF)
            dk = jnp.dot(ds, qb, preferred_element_type=jnp.float32)
            dv = jnp.dot(p.astype(jnp.bfloat16), dob, preferred_element_type=jnp.float32)
            dkw[n, to] = dk.reshape(size // HALF, HALF, HD)
            dvw[n, to] = dv.reshape(size // HALF, HALF, HD)
            dq = dq + dot_tn(tile(kpos, off, size), ds)
        dq = (dq * SCALE).T.astype(jnp.bfloat16)
        for i in range(GROUP):
            dq_v[xs, rows, i * HD:(i + 1) * HD] = dq[i * HALF:(i + 1) * HALF]

    copies = []

    def attend(d):
        if d:
            for j in range(2):
                qd[NX - d, j].wait_recv()
        else:
            loads[3].wait()
            loads[4].wait()

        def side(j, carry):
            row_block(d, j)
            return carry

        lax.fori_loop(0, 2, side, 0)
        if d:
            px = wrap(x + d, NX)
            copy = remote(dq_v.at[px], dq_got.at[x], (dq_send, dq_recv), d - 1, (wide, px * NZ + zl))
            copy.start()
            copies.append(copy)

    attend(0)
    near.advance(3)
    attend(1)

    @pl.when(line.inner)
    def _():
        to_inner.wait_recv()

    @pl.when(line.edge)
    def _():
        to_across.wait_send()
        to_inner.wait_send()

    near.advance(4)
    far.begin()
    attend(3)
    far.begin_second()
    attend(2)
    far.advance(1)

    blocks = [map_ref[j, wrap(x + d, NX) * NZ + zl] for d in range(NX) for j in range(2)]

    def terms_of(z):
        def one(xs, carry):
            slot = z * NX + xs
            for j in range(2):
                p = map_ref[j, xs * NZ + z]
                sums = [jnp.zeros((HALF, HD), jnp.float32)] * 2
                for n, block in enumerate(blocks):
                    step = p - block + BACK
                    inside = (step >= 0) & (step <= BACK)
                    at = jnp.minimum(jnp.maximum(step, 0), BACK)
                    sums = [a + jnp.where(inside, b[n, at], 0.0) for a, b in zip(sums, (dkw, dvw))]
                rows = pl.ds(j * HALF, HALF)
                terms_v[slot, 0, rows] = (sums[0] * SCALE).astype(jnp.bfloat16)
                terms_v[slot, 1, rows] = sums[1].astype(jnp.bfloat16)
            return carry

        lax.fori_loop(0, NX, one, 0)

    def far_term(n, d):
        return terms_v.at[far_z[n] * NX + wrap(x + d, NX)]

    def pass_copy(n, d):
        return remote(far_term(n, d), passed.at[n, d], (pass_send, pass_recv), 2 * d + n, partner)

    def sum_copy(n, d):
        return remote(far_term(n, d), terms_got.at[2, x], (sum_send, sum_recv), 2 * d + n,
                      (wide, wrap(x + d, NX) * NZ + far_z[n]))

    for n in range(2):
        terms_of(far_z[n])

        @pl.when(line.edge)
        def _():
            for d in range(NX):
                pass_copy(n, d).start()

    terms_of(line.partner)
    for d in range(NX):
        px = wrap(x + d, NX)
        copy = remote(terms_v.at[line.partner * NX + px], terms_got.at[1, x], (t_send, t_recv), d,
                      (wide, px * NZ + line.partner))
        copy.start()
        copies.append(copy)
    terms_of(zl)
    for d in (2, 1, 3):
        px = wrap(x + d, NX)
        copy = remote(terms_v.at[zl * NX + px], terms_got.at[0, x], (t_send, t_recv), 3 + d, (wide, px * NZ + zl))
        copy.start()
        copies.append(copy)
    stores = [
        pltpu.make_async_copy(dq_v.at[x], dq_got.at[x], local_sem.at[6]),
        pltpu.make_async_copy(terms_v.at[own_slot], terms_got.at[0, x], local_sem.at[7]),
    ]
    for copy in stores:
        copy.start()

    def combine(n):
        @pl.when(line.inner)
        def _():
            for d in range(NX):
                pass_copy(n, d).wait_recv()
                slot = far_z[n] * NX + wrap(x + d, NX)
                total = terms_v[slot].astype(jnp.float32) + passed[n, d].astype(jnp.float32)
                terms_v[slot] = total.astype(jnp.bfloat16)
                sum_copy(n, d).start()

    combine(0)
    far.advance(2)
    combine(1)
    loads[5].wait()
    near.wait_core(near.core_copies)
    lax.fori_loop(0, NY, project_near, 0)
    far.advance(3)
    far.wait_core(far.core_copies[:10])
    lax.fori_loop(0, 5, project_far, 0)
    far.advance(4)
    far.wait_core(far.core_copies[10:])
    lax.fori_loop(5, NY, project_far, 0)
    projected[...] = acc[...].astype(jnp.bfloat16)
    for copy in copies:
        copy.wait()
    own_kind = (zl // 2 + zl % 2 + 1) % 2
    for d in range(NX):
        remote(passed.at[0, d], passed.at[0, d], (sum_send, sum_recv), 2 * d + own_kind, partner).wait_recv()

    @pl.when(line.edge)
    def _():
        for d in range(NX):
            for n in range(2):
                pass_copy(n, d).wait_send()

    @pl.when(line.inner)
    def _():
        for d in range(NX):
            for n in range(2):
                relay_copy(n, d).wait_send()
                sum_copy(n, d).wait_send()

    for copy in list(kx.values()) + kz + list(qd.values()):
        copy.wait_send()
    near.finish_sends()
    far.finish_sends()
    for copy in stores:
        copy.wait()


def finish_kernel(dq_got, terms_got, projected, dq, dk, dv, kref, vref, dq_v, terms_v, sems):
    x_load = pltpu.make_async_copy(dq_got, dq_v, sems.at[0])
    t_load = pltpu.make_async_copy(terms_got, terms_v, sems.at[1])
    x_load.start()
    t_load.start()
    kref[0] = projected[:, :512]
    vref[0] = projected[:, 512:]
    x_load.wait()
    for xs in range(NX):
        dq[0, :, xs * 512:(xs + 1) * 512] = dq_v[xs].astype(jnp.float32)
    t_load.wait()
    for xs in range(NX):
        for j, out in enumerate((dk, dv)):
            total = terms_v[0, xs, j].astype(jnp.float32)
            for n in (1, 2):
                total = total + terms_v[n, xs, j].astype(jnp.float32)
            out[0, :, xs * HD:(xs + 1) * HD] = total


def body(q_pol, k_pol, v_pol, d_out, h_ref, norm_gain, w_kv_ref, lengths, block_map):
    bf16, f32 = jnp.bfloat16, jnp.float32
    hbm = pl.BlockSpec(memory_space=pltpu.HBM)
    vmem = pl.BlockSpec(memory_space=pltpu.VMEM)
    smem = pl.BlockSpec(memory_space=pltpu.SMEM)
    dma = pltpu.SemaphoreType.DMA
    shape = jax.ShapeDtypeStruct
    heads = (NX, ROWS, GROUP * HD)
    dq_got, terms_got, projected = pl.pallas_call(
        step_kernel,
        name="step",
        out_shape=(shape(heads, bf16), shape((3, NX, 2, ROWS, HD), bf16), shape((ROWS, 1024), bf16)),
        in_specs=[smem, smem] + [hbm] * 6 + [vmem],
        out_specs=(hbm, hbm, vmem),
        scratch_shapes=[
            pltpu.VMEM(heads, bf16),
            pltpu.VMEM(heads, bf16),
            pltpu.VMEM((NX * NZ, 2, ROWS, HD), bf16),
            pltpu.VMEM((BACK + 2 * NX * NZ, HALF, HD), bf16),
            pltpu.VMEM((BACK + 2 * NX * NZ, HALF, HD), bf16),
            pltpu.VMEM((WINDOW, GROUP * HALF), f32),
            pltpu.VMEM((WINDOW, GROUP * HALF), f32),
            pltpu.VMEM((2 * NX, BACK + 1, HALF, HD), f32),
            pltpu.VMEM((2 * NX, BACK + 1, HALF, HD), f32),
            pltpu.VMEM((NX * NZ, 2, ROWS, HD), bf16),
            pltpu.VMEM(heads, bf16),
            pltpu.VMEM((2, NX, 2, ROWS, HD), bf16),
            pltpu.VMEM((NY, 2 * ROWS, 1024), bf16),
            pltpu.VMEM((NY, 2 * ROWS, 1024), bf16),
            pltpu.VMEM((ROWS, 4096), bf16),
            pltpu.VMEM((ROWS, 4096), bf16),
            pltpu.VMEM((ROWS, 1024), f32),
        ]
        + [dma((n,)) for n in (6, 6, 6, 6, 8, 16, 8, 2, 2, 3, 3, 7, 7, 8, 8, 8, 8, 16, 16, 18, 18, 16, 16, 18, 18, 8)],
        compiler_params=pltpu.CompilerParams(collective_id=0, has_side_effects=True, vmem_limit_bytes=VMEM_ALL),
    )(block_map.T, lengths, q_pol, k_pol, v_pol, d_out, w_kv_ref, h_ref, norm_gain.reshape(1, -1))
    return pl.pallas_call(
        finish_kernel,
        name="finish",
        out_shape=(
            shape((1, ROWS, 2048), f32),
            shape((1, ROWS, 512), f32),
            shape((1, ROWS, 512), f32),
            shape((1, ROWS, 512), bf16),
            shape((1, ROWS, 512), bf16),
        ),
        in_specs=[hbm, hbm, vmem],
        out_specs=(vmem,) * 5,
        scratch_shapes=[pltpu.VMEM(heads, bf16), pltpu.VMEM((3, NX, 2, ROWS, HD), bf16), dma((2,))],
        compiler_params=pltpu.CompilerParams(vmem_limit_bytes=VMEM_ALL),
    )(dq_got, terms_got, projected)


def solution(mesh):
    rows = P("wide", "ctx", None)
    return jax.shard_map(
        body,
        mesh=mesh,
        in_specs=(rows, rows, rows, rows, rows, P(), P("wide", None), P("wide", None), P()),
        out_specs=(rows,) * 5,
        check_vma=False,
    )
```

time: 105 us -> 79.7 us (0.76)
  Pallas kernels: 94.1 us -> 77.5 us
  local copies, waits for them, and re-layouts: 10.1 us -> 1.31 us
    pallas_call x3 -> x2, Pallas kernels: 94.1 us -> 77.5 us  [the longest x1 74 us: body(): pl.pallas_call(step_kernel, name='step', out_shape=(shape(heads, bf16), s...]
    unnamed x18 -> x0, local copies, waits for them, and re-layouts: 9.35 us -> none
where the time goes in v2:
time: 79.7 us; the launch traced here: 79.4 us
  Pallas kernels  77.5 us (97%)
  local copies, waits for them, and re-layouts  1.31 us (2%)
    pallas_call x1, Pallas kernels, body(): pl.pallas_call(step_kernel, name='step', out_shape=(shape(heads, bf16), s...  74 us
    pallas_call x1, Pallas kernels, body(): pl.pallas_call(finish_kernel, name='finish', out_shape=(shape((1, ROWS, 2...  3.48 us

profile of v2, /device:TPU:1, one launch (start us, length us, event | category | flops | bytes accessed | tf_op | source)
XLA Modules:
  0.0 79.4 jit_solution(15167113527323330428)
XLA Ops:
  0.6 1.3 %reshape.13.gain = bf16[1,4096]{1,0:T(2,128)(2,1)} reshape(bf16[4096]{0:T(1024)(128)(2,1)} %param.14) | data formatting | bytes 16384 | tf_op jit(solution)/shard_map/reshape | solution.py:583
  1.9 74.0 %step.1 = (bf16[4,128,512]{2,1,0:T(8,128)(2,1)}, bf16[3,4,2,128,128]{4,3,2,1,0:T(8,128)(2,1)}, bf16[128,1024]{1,0:T(8,128)(2,1)}) custom-call(s32[2,16]{1,0:T(2,128)} %bitcast.1, s32[1,4]{1,0:T(1,128)} %len_ref.1, bf16[1,128,2048]{2,1,0:T(8,128)(2,1)} %q.1, bf16[1,128,512]{2,1,0:T(8,128)(2,1)} %k.1, bf16[1,128,512]{2,1,0:T(8,128)(2,1)} %v.1, ...), custom_call_target="tpu_custom_call" | custom-call | tf_op jit(solution)/shard_map/step/pallas_call | solution.py:556
  76.0 3.5 %finish.1 = (f32[1,128,2048]{2,1,0:T(8,128)}, f32[1,128,512]{2,1,0:T(8,128)}, f32[1,128,512]{2,1,0:T(8,128)}, bf16[1,128,512]{2,1,0:T(8,128)(2,1)}, bf16[1,128,512]{2,1,0:T(8,128)(2,1)}) custom-call(bf16[4,128,512]{2,1,0:T(8,128)(2,1)} %get-tuple-element.8.dq_got, bf16[3,4,2,128,128]{4,3,2,1,0:T(8,128)(2,1)} %get-tuple-element.9.terms_got, ...), custom_call_target="tpu_custom_call" | custom-call | tf_op jit(solution)/shard_map/finish/pallas_call | solution.py:584

commit v3 on v2

--- a/solution.py
+++ b/solution.py
@@ -274,18 +274,28 @@
     relay(1)
     loads[2].wait()
     strip = 16
+    scale_by = gain[...].astype(jnp.float32)
 
     def norm_rows(i, carry):
         rows = pl.ds(pl.multiple_of(i * strip, strip), strip)
         a = h_v[rows].astype(jnp.float32)
         mean = jnp.mean(a * a, axis=1, keepdims=True)
-        normed[rows] = (a * lax.rsqrt(mean + 1e-05) * gain[...].astype(jnp.float32)).astype(jnp.bfloat16)
+        a = a * lax.rsqrt(mean + 1e-05)
+        for c in range(a.shape[1] // HD):
+            at = slice(c * HD, (c + 1) * HD)
+            normed[rows, at] = (a[:, at] * scale_by[c:c + 1]).astype(jnp.bfloat16)
         return carry
 
     lax.fori_loop(0, ROWS // strip, norm_rows, 0)
     acc[...] = jnp.zeros_like(acc)
     near.advance(2)
     relay(2)
+
+    @pl.when(line.inner)
+    def _():
+        to_inner.wait_recv()
+
+    far.begin()
 
     def project(weights, zh_of, owner):
         at = pl.ds(pl.multiple_of((2 * owner + zh_of) * 2 * ROWS, 2 * ROWS), 2 * ROWS)
@@ -400,23 +410,18 @@
 
     attend(0)
     near.advance(3)
+    far.begin_second()
     attend(1)
-
-    @pl.when(line.inner)
-    def _():
-        to_inner.wait_recv()
+    far.advance(1)
+    attend(3)
+    near.advance(4)
+    attend(2)
+    far.advance(2)
 
     @pl.when(line.edge)
     def _():
         to_across.wait_send()
         to_inner.wait_send()
-
-    near.advance(4)
-    far.begin()
-    attend(3)
-    far.begin_second()
-    attend(2)
-    far.advance(1)
 
     blocks = [map_ref[j, wrap(x + d, NX) * NZ + zl] for d in range(NX) for j in range(2)]
 
@@ -486,13 +491,12 @@
                 terms_v[slot] = total.astype(jnp.bfloat16)
                 sum_copy(n, d).start()
 
-    combine(0)
-    far.advance(2)
-    combine(1)
     loads[5].wait()
     near.wait_core(near.core_copies)
     lax.fori_loop(0, NY, project_near, 0)
+    combine(0)
     far.advance(3)
+    combine(1)
     far.wait_core(far.core_copies[:10])
     lax.fori_loop(0, 5, project_far, 0)
     far.advance(4)
@@ -526,23 +530,41 @@
         copy.wait()
 
 
-def finish_kernel(dq_got, terms_got, projected, dq, dk, dv, kref, vref, dq_v, terms_v, sems):
-    x_load = pltpu.make_async_copy(dq_got, dq_v, sems.at[0])
-    t_load = pltpu.make_async_copy(terms_got, terms_v, sems.at[1])
-    x_load.start()
+def finish_kernel(dq_got, terms_got, projected, dq, dk, dv, kref, vref,
+                  dq_v, terms_v, p_v, dq_f, dkv_f, kv_f, load_sems, store_sems):
+    x_loads = [pltpu.make_async_copy(dq_got.at[xs], dq_v.at[xs], load_sems.at[xs]) for xs in range(NX)]
+    t_load = pltpu.make_async_copy(terms_got, terms_v, load_sems.at[NX])
+    p_load = pltpu.make_async_copy(projected, p_v, load_sems.at[NX + 1])
+    stores = []
+
+    def store(src, dst):
+        copy = pltpu.make_async_copy(src, dst, store_sems.at[len(stores)])
+        copy.start()
+        stores.append(copy)
+
+    for copy in x_loads:
+        copy.start()
     t_load.start()
-    kref[0] = projected[:, :512]
-    vref[0] = projected[:, 512:]
-    x_load.wait()
+    p_load.start()
     for xs in range(NX):
-        dq[0, :, xs * 512:(xs + 1) * 512] = dq_v[xs].astype(jnp.float32)
+        x_loads[xs].wait()
+        at = pl.ds(xs * GROUP * HD, GROUP * HD)
+        dq_f[xs] = dq_v[xs].astype(jnp.float32)
+        store(dq_f.at[xs], dq.at[0, :, at])
     t_load.wait()
-    for xs in range(NX):
-        for j, out in enumerate((dk, dv)):
+    for j, out in enumerate((dk, dv)):
+        for xs in range(NX):
             total = terms_v[0, xs, j].astype(jnp.float32)
             for n in (1, 2):
                 total = total + terms_v[n, xs, j].astype(jnp.float32)
-            out[0, :, xs * HD:(xs + 1) * HD] = total
+            dkv_f[j, :, xs * HD:(xs + 1) * HD] = total
+        store(dkv_f.at[j], out.at[0])
+    p_load.wait()
+    for j, out in enumerate((kref, vref)):
+        kv_f[j] = p_v[:, j * 512:(j + 1) * 512]
+        store(kv_f.at[j], out.at[0])
+    for copy in stores:
+        copy.wait()
 
 
 def body(q_pol, k_pol, v_pol, d_out, h_ref, norm_gain, w_kv_ref, lengths, block_map):
@@ -580,7 +602,7 @@
         ]
         + [dma((n,)) for n in (6, 6, 6, 6, 8, 16, 8, 2, 2, 3, 3, 7, 7, 8, 8, 8, 8, 16, 16, 18, 18, 16, 16, 18, 18, 8)],
         compiler_params=pltpu.CompilerParams(collective_id=0, has_side_effects=True, vmem_limit_bytes=VMEM_ALL),
-    )(block_map.T, lengths, q_pol, k_pol, v_pol, d_out, w_kv_ref, h_ref, norm_gain.reshape(1, -1))
+    )(block_map.T, lengths, q_pol, k_pol, v_pol, d_out, w_kv_ref, h_ref, norm_gain.reshape(-1, HD))
     return pl.pallas_call(
         finish_kernel,
         name="finish",
@@ -591,9 +613,18 @@
             shape((1, ROWS, 512), bf16),
             shape((1, ROWS, 512), bf16),
         ),
-        in_specs=[hbm, hbm, vmem],
-        out_specs=(vmem,) * 5,
-        scratch_shapes=[pltpu.VMEM(heads, bf16), pltpu.VMEM((3, NX, 2, ROWS, HD), bf16), dma((2,))],
+        in_specs=[hbm] * 3,
+        out_specs=(hbm,) * 5,
+        scratch_shapes=[
+            pltpu.VMEM(heads, bf16),
+            pltpu.VMEM((3, NX, 2, ROWS, HD), bf16),
+            pltpu.VMEM((ROWS, 1024), bf16),
+            pltpu.VMEM(heads, f32),
+            pltpu.VMEM((2, ROWS, 512), f32),
+            pltpu.VMEM((2, ROWS, 512), bf16),
+            dma((NX + 2,)),
+            dma((NX + 4,)),
+        ],
         compiler_params=pltpu.CompilerParams(vmem_limit_bytes=VMEM_ALL),
     )(dq_got, terms_got, projected)
 

time: 79.7 us -> 73.5 us (0.922)
  Pallas kernels: 77.5 us -> 72.1 us
  local copies, waits for them, and re-layouts: 1.31 us -> 0 us
    pallas_call x1, Pallas kernels: 74 us -> 69.7 us  [body(): pl.pallas_call(step_kernel, name='step', out_shape=(shape(heads, bf16), s...]
    reshape x1 -> x0, local copies, waits for them, and re-layouts: 1.31 us -> none  [body(): norm_gain.reshape(1, -1)]
    pallas_call x1, Pallas kernels: 3.48 us -> 2.44 us  [body(): pl.pallas_call(finish_kernel, name='finish', out_shape=(shape((1, ROWS, 2...]
where the time goes in v3:
time: 73.5 us; the launch traced here: 72.8 us
  Pallas kernels  72.1 us (98%)
    pallas_call x1, Pallas kernels, body(): pl.pallas_call(step_kernel, name='step', out_shape=(shape(heads, bf16), s...  69.7 us
    pallas_call x1, Pallas kernels, body(): pl.pallas_call(finish_kernel, name='finish', out_shape=(shape((1, ROWS, 2...  2.44 us

profile of v3, /device:TPU:1, one launch (start us, length us, event | category | flops | bytes accessed | tf_op | source)
XLA Modules:
  0.0 72.8 jit_solution(11618625069477591465)
XLA Ops:
  0.6 69.7 %step.1 = (bf16[4,128,512]{2,1,0:T(8,128)(2,1)}, bf16[3,4,2,128,128]{4,3,2,1,0:T(8,128)(2,1)}, bf16[128,1024]{1,0:T(8,128)(2,1)}) custom-call(s32[2,16]{1,0:T(2,128)} %bitcast.3, s32[1,4]{1,0:T(1,128)} %len_ref.1, bf16[1,128,2048]{2,1,0:T(8,128)(2,1)} %q.1, bf16[1,128,512]{2,1,0:T(8,128)(2,1)} %k.1, bf16[1,128,512]{2,1,0:T(8,128)(2,1)} %v.1, ...), custom_call_target="tpu_custom_call" | custom-call | tf_op jit(solution)/shard_map/step/pallas_call | solution.py:578
  70.3 2.4 %finish.1 = (f32[1,128,2048]{2,1,0:T(8,128)}, f32[1,128,512]{2,1,0:T(8,128)}, f32[1,128,512]{2,1,0:T(8,128)}, bf16[1,128,512]{2,1,0:T(8,128)(2,1)}, bf16[1,128,512]{2,1,0:T(8,128)(2,1)}) custom-call(bf16[4,128,512]{2,1,0:T(8,128)(2,1)} %get-tuple-element.8.dq_got, bf16[3,4,2,128,128]{4,3,2,1,0:T(8,128)(2,1)} %get-tuple-element.9.terms_got, ...), custom_call_target="tpu_custom_call" | custom-call | tf_op jit(solution)/shard_map/finish/pallas_call | solution.py:606

commit v4 on v3

--- a/solution.py
+++ b/solution.py
@@ -106,20 +106,13 @@
         return step < 4 or (step == 4 and part == way)
 
     def begin(self):
-        for way in range(2):
-            copy = self.ring_copy(way, 1, 0)
-            copy.start()
-            self.sent.append(copy)
+        for part in range(2):
+            for way in range(2):
+                copy = self.ring_copy(way, 1, part)
+                copy.start()
+                self.sent.append(copy)
         for part in range(2):
             self.to_core(self.own.at[pl.ds(part * HALF, HALF)], self.y, part, part)
-
-    def begin_second(self):
-        for copy in self.sent[:2]:
-            copy.wait_send()
-        for way in range(2):
-            copy = self.ring_copy(way, 1, 1)
-            copy.start()
-            self.sent.append(copy)
 
     def advance(self, step):
         for part in range(2):
@@ -139,7 +132,7 @@
             remote(dst, dst, self.core_sems, slot, self.other).wait_recv()
 
     def finish_sends(self):
-        for copy in self.sent[2:]:
+        for copy in self.sent:
             copy.wait_send()
         for copy, _, _, _ in self.core_copies:
             copy.wait_send()
@@ -175,7 +168,7 @@
 
 
 def step_kernel(map_ref, len_ref, q, k, v, do, w, h, gain, dq_got, terms_got, projected,
-                q_v, do_v, kv_v, kpos, vpos, s_ref, g_ref, dkw, dvw, terms_v, dq_v, passed,
+                q_v, do_v, kv_v, kpos, vpos, s_ref, g_ref, s2_ref, g2_ref, dkw, dvw, terms_v, dq_v, passed,
                 near_v, far_v, h_v, normed, acc,
                 x_send, x_recv, kx_send, kx_recv, kz_send, kz_recv, relay_send, zh_send, zh_recv,
                 dq_send, dq_recv, t_send, t_recv, pass_send, pass_recv, sum_send, sum_recv,
@@ -259,12 +252,11 @@
                               (wide, px * NZ + zl))
             qd[d, j].start()
     relay(0)
-    near.begin_second()
 
     kpos[pl.ds(0, BACK)] = jnp.zeros((BACK, HALF, HD), jnp.bfloat16)
     vpos[pl.ds(0, BACK)] = jnp.zeros((BACK, HALF, HD), jnp.bfloat16)
+    near.advance(1)
     relay(3)
-    near.advance(1)
 
     @pl.when(line.edge)
     def _():
@@ -329,6 +321,7 @@
         return carry
 
     lax.fori_loop(0, NX * NZ, place_block, 0)
+    near.advance(3)
     ends = [len_ref[0, 0]]
     for i in range(1, 4):
         ends.append(ends[-1] + len_ref[0, i])
@@ -339,84 +332,116 @@
             start = jnp.where(pos >= end, end, start)
         return start
 
-    def row_block(d, j):
-        xs = wrap(x + d, NX)
-        n = 2 * d + j
-        block = map_ref[j, xs * NZ + zl]
-        base = block * HALF
-        rows = pl.ds(pl.multiple_of(j * HALF, HALF), HALF)
-        qb = jnp.concatenate([q_v[xs, rows, i * HD:(i + 1) * HD] for i in range(GROUP)], axis=0)
-        dob = jnp.concatenate([do_v[xs, rows, i * HD:(i + 1) * HD] for i in range(GROUP)], axis=0)
-        lane = lax.broadcasted_iota(jnp.int32, (1, GROUP * HALF), 1)
-        pos = base + lane % HALF
-        first = doc_start(pos)
-        top = jnp.full((8, GROUP * HALF), NEG, jnp.float32)
-
-        def tile(ref, off, size):
-            first_block = block + (WINDOW - off - size) // HALF
-            parts = [ref[first_block + i] for i in range(size // HALF)]
+    class Block:
+        def __init__(self, d, j, buffers):
+            self.xs, self.n = wrap(x + d, NX), 2 * d + j
+            self.rows = slice(j * HALF, (j + 1) * HALF)
+            self.s, self.g = buffers
+            self.block = map_ref[j, self.xs * NZ + zl]
+            self.base = self.block * HALF
+            self.q = self.heads(q_v)
+            self.do = self.heads(do_v)
+            lane = lax.broadcasted_iota(jnp.int32, (1, GROUP * HALF), 1)
+            self.pos = self.base + lane % HALF
+            self.first = doc_start(self.pos)
+            self.top = jnp.full((8, GROUP * HALF), NEG, jnp.float32)
+            self.total = jnp.zeros((8, GROUP * HALF), jnp.float32)
+            self.delta = jnp.zeros((8, GROUP * HALF), jnp.float32)
+            self.dq = jnp.zeros((HD, GROUP * HALF), jnp.float32)
+
+        def heads(self, ref):
+            return jnp.concatenate([ref[self.xs, self.rows, i * HD:(i + 1) * HD] for i in range(GROUP)], axis=0)
+
+        def tile(self, ref, off, size):
+            start = self.block + (WINDOW - off - size) // HALF
+            parts = [ref[start + i] for i in range(size // HALF)]
             return jnp.concatenate(parts, axis=0) if len(parts) > 1 else parts[0]
 
-        for off, size in TILES:
-            kp = base + HALF - off - size + lax.broadcasted_iota(jnp.int32, (size, GROUP * HALF), 0)
-            s = jnp.where((kp <= pos) & (kp >= first), dot_nt(tile(kpos, off, size), qb), NEG)
-            s_ref[off:off + size] = s
-            g_ref[off:off + size] = dot_nt(tile(vpos, off, size), dob)
-            top = jnp.maximum(top, fold(s, jnp.maximum))
-        top = jnp.max(top, axis=0, keepdims=True)
-        total = jnp.zeros((8, GROUP * HALF), jnp.float32)
-        delta = jnp.zeros((8, GROUP * HALF), jnp.float32)
-        for off, size in TILES:
-            p = jnp.exp2((s_ref[off:off + size] - top) * (SCALE * LOG2E))
-            s_ref[off:off + size] = p
-            total = total + fold(p, jnp.add)
-            delta = delta + fold(p * g_ref[off:off + size], jnp.add)
-        inverse = 1.0 / jnp.sum(total, axis=0, keepdims=True)
-        delta = jnp.sum(delta, axis=0, keepdims=True) * inverse
-        dq = jnp.zeros((HD, GROUP * HALF), jnp.float32)
-        for off, size in TILES:
-            p = s_ref[off:off + size] * inverse
-            ds = (p * (g_ref[off:off + size] - delta)).astype(jnp.bfloat16)
+        def score(self, off, size):
+            kp = self.base + HALF - off - size + lax.broadcasted_iota(jnp.int32, (size, GROUP * HALF), 0)
+            seen = kp >= self.first
+            if off == 0:
+                seen = seen & (kp <= self.pos)
+            s = jnp.where(seen, dot_nt(self.tile(kpos, off, size), self.q), NEG)
+            self.s[off:off + size] = s
+            self.g[off:off + size] = dot_nt(self.tile(vpos, off, size), self.do)
+            self.top = jnp.maximum(self.top, fold(s, jnp.maximum))
+
+        def start_weigh(self):
+            self.top = jnp.max(self.top, axis=0, keepdims=True)
+
+        def weigh(self, off, size):
+            p = jnp.exp2((self.s[off:off + size] - self.top) * (SCALE * LOG2E))
+            self.s[off:off + size] = p
+            self.total = self.total + fold(p, jnp.add)
+            self.delta = self.delta + fold(p * self.g[off:off + size], jnp.add)
+
+        def start_grads(self):
+            self.inverse = 1.0 / jnp.sum(self.total, axis=0, keepdims=True)
+            self.delta = jnp.sum(self.delta, axis=0, keepdims=True) * self.inverse
+
+        def grads(self, off, size):
+            p = self.s[off:off + size] * self.inverse
+            ds = (p * (self.g[off:off + size] - self.delta)).astype(jnp.bfloat16)
             to = pl.ds((WINDOW - off - size) // HALF, size // HALF)
-            dk = jnp.dot(ds, qb, preferred_element_type=jnp.float32)
-            dv = jnp.dot(p.astype(jnp.bfloat16), dob, preferred_element_type=jnp.float32)
-            dkw[n, to] = dk.reshape(size // HALF, HALF, HD)
-            dvw[n, to] = dv.reshape(size // HALF, HALF, HD)
-            dq = dq + dot_tn(tile(kpos, off, size), ds)
-        dq = (dq * SCALE).T.astype(jnp.bfloat16)
-        for i in range(GROUP):
-            dq_v[xs, rows, i * HD:(i + 1) * HD] = dq[i * HALF:(i + 1) * HALF]
+            dk = jnp.dot(ds, self.q, preferred_element_type=jnp.float32)
+            dv = jnp.dot(p.astype(jnp.bfloat16), self.do, preferred_element_type=jnp.float32)
+            dkw[self.n, to] = dk.reshape(size // HALF, HALF, HD)
+            dvw[self.n, to] = dv.reshape(size // HALF, HALF, HD)
+            self.dq = self.dq + dot_tn(self.tile(kpos, off, size), ds)
+
+        def store(self):
+            dq = (self.dq * SCALE).T.astype(jnp.bfloat16)
+            for i in range(GROUP):
+                dq_v[self.xs, self.rows, i * HD:(i + 1) * HD] = dq[i * HALF:(i + 1) * HALF]
 
     copies = []
 
-    def attend(d):
+    def lower_block(d):
         if d:
             for j in range(2):
                 qd[NX - d, j].wait_recv()
         else:
             loads[3].wait()
             loads[4].wait()
-
-        def side(j, carry):
-            row_block(d, j)
-            return carry
-
-        lax.fori_loop(0, 2, side, 0)
+        return Block(d, 0, (s_ref, g_ref))
+
+    def serve(m):
+        if m == 1:
+            far.advance(1)
+        elif m == 2:
+            near.advance(4)
+
+    order = (0, 1, 3, 2)
+    lower = lower_block(0)
+    for t in TILES:
+        lower.score(*t)
+    for m, d in enumerate(order):
+        upper = Block(d, 1, (s2_ref, g2_ref))
+        lower.start_weigh()
+        for t in TILES:
+            lower.weigh(*t)
+            upper.score(*t)
+        lower.start_grads()
+        upper.start_weigh()
+        for t in TILES:
+            lower.grads(*t)
+            upper.weigh(*t)
+        lower.store()
+        upper.start_grads()
+        after = lower_block(order[m + 1]) if m + 1 < NX else None
+        for t in TILES:
+            upper.grads(*t)
+            if after is not None:
+                after.score(*t)
+        upper.store()
+        lower = after
         if d:
             px = wrap(x + d, NX)
             copy = remote(dq_v.at[px], dq_got.at[x], (dq_send, dq_recv), d - 1, (wide, px * NZ + zl))
             copy.start()
             copies.append(copy)
-
-    attend(0)
-    near.advance(3)
-    far.begin_second()
-    attend(1)
-    far.advance(1)
-    attend(3)
-    near.advance(4)
-    attend(2)
-    far.advance(2)
+        serve(m)
 
     @pl.when(line.edge)
     def _():
@@ -491,6 +516,7 @@
                 terms_v[slot] = total.astype(jnp.bfloat16)
                 sum_copy(n, d).start()
 
+    far.advance(2)
     loads[5].wait()
     near.wait_core(near.core_copies)
     lax.fori_loop(0, NY, project_near, 0)
@@ -587,6 +613,8 @@
             pltpu.VMEM((NX * NZ, 2, ROWS, HD), bf16),
             pltpu.VMEM((BACK + 2 * NX * NZ, HALF, HD), bf16),
             pltpu.VMEM((BACK + 2 * NX * NZ, HALF, HD), bf16),
+            pltpu.VMEM((WINDOW, GROUP * HALF), f32),
+            pltpu.VMEM((WINDOW, GROUP * HALF), f32),
             pltpu.VMEM((WINDOW, GROUP * HALF), f32),
             pltpu.VMEM((WINDOW, GROUP * HALF), f32),
             pltpu.VMEM((2 * NX, BACK + 1, HALF, HD), f32),

time: 73.5 us -> 68.3 us (0.929)
  the two profiles are of different devices: /device:TPU:1 before, /device:TPU:6 now
where the time goes in v4:
time: 68.3 us; the launch traced here: 68.1 us
  Pallas kernels  67.5 us (99%)
    pallas_call x1, Pallas kernels, body(): pl.pallas_call(step_kernel, name='step', out_shape=(shape(heads, bf16), s...  65 us
    pallas_call x1, Pallas kernels, body(): pl.pallas_call(finish_kernel, name='finish', out_shape=(shape((1, ROWS, 2...  2.44 us

profile of v4, /device:TPU:6, one launch (start us, length us, event | category | flops | bytes accessed | tf_op | source)
XLA Modules:
  0.0 68.1 jit_solution(5756688731355453764)
XLA Ops:
  0.6 65.0 %step.1 = (bf16[4,128,512]{2,1,0:T(8,128)(2,1)}, bf16[3,4,2,128,128]{4,3,2,1,0:T(8,128)(2,1)}, bf16[128,1024]{1,0:T(8,128)(2,1)}) custom-call(s32[2,16]{1,0:T(2,128)} %bitcast.3, s32[1,4]{1,0:T(1,128)} %len_ref.1, bf16[1,128,2048]{2,1,0:T(8,128)(2,1)} %q.1, bf16[1,128,512]{2,1,0:T(8,128)(2,1)} %k.1, bf16[1,128,512]{2,1,0:T(8,128)(2,1)} %v.1, ...), custom_call_target="tpu_custom_call" | custom-call | tf_op jit(solution)/shard_map/step/pallas_call | solution.py:604
  65.7 2.4 %finish.1 = (f32[1,128,2048]{2,1,0:T(8,128)}, f32[1,128,512]{2,1,0:T(8,128)}, f32[1,128,512]{2,1,0:T(8,128)}, bf16[1,128,512]{2,1,0:T(8,128)(2,1)}, bf16[1,128,512]{2,1,0:T(8,128)(2,1)}) custom-call(bf16[4,128,512]{2,1,0:T(8,128)(2,1)} %get-tuple-element.8.dq_got, bf16[3,4,2,128,128]{4,3,2,1,0:T(8,128)(2,1)} %get-tuple-element.9.terms_got, ...), custom_call_target="tpu_custom_call" | custom-call | tf_op jit(solution)/shard_map/finish/pallas_call | solution.py:634
